TPU v7x, 32 devices: a whole 2x2x4 slice. The times are simulated.
32 devices in a mesh: seq: 8 (over z, x), ch: 4 (over y, core).
Axes of the slice: x: 2, y: 2, z: 4, core: 2. Of those that a mesh axis runs over, the one named last changes fastest.
Arguments:
- block_input: bfloat16 [8192, 2048], P('ch', 'seq'), may hold values from -110 to 110
- norm_gain: float32 [8192], P('ch'), may hold values from 0.1 to 1.9
- short_taps: bfloat16 [8192, 7], P('ch'), may hold values from -2 to 2
- medium_taps: bfloat16 [8192, 128], P('ch'), may hold values from -0.5 to 0.5
- long_filter: float32 [8192, 2048], P(('ch', 'seq')), may hold values from -2 to 2
- grad_out: bfloat16 [8192, 2048], P('ch', 'seq'), may hold values from -2.390625 to 2.390625
Outputs:
- grad_normed: bfloat16 [8192, 2048], P('ch', 'seq')
- grad_long: float32 [8192, 2048], P(('ch', 'seq'))
- grad_medium: float32 [8192, 128], P(('ch', 'seq'))
- grad_short: float32 [8192, 7], P(('ch', 'seq'))
All inputs are finite; a program needn't handle non-finite values.
Results may differ from a plain program's by a relative error of at most 0.0058.
Values may be sent and summed in bfloat16 or wider, within the bound.
A program may use at most 128 MiB of HBM per device.

v0:
```python
import math

import jax
import jax.numpy as jnp
from jax import lax
from jax.sharding import PartitionSpec as P

highest = lax.Precision.HIGHEST


def depthwise(signal, taps):
    result = lax.conv_general_dilated(
        signal[None],
        taps[:, None, :],
        (1,),
        "VALID",
        dimension_numbers=("NCH", "OIH", "NCH"),
        feature_group_count=signal.shape[0],
        preferred_element_type=jnp.float32,
    )
    return result[0]


def fourier_tables(length):
    total = 2 * length
    inner = 128
    outer = total // inner
    half = outer // 2
    two_pi = 2.0 * math.pi
    freq_outer = jnp.arange(outer, dtype=jnp.int32)
    pos_half = jnp.arange(half, dtype=jnp.int32)
    pos_inner = jnp.arange(inner, dtype=jnp.int32)
    outer_angle = (
        two_pi * (freq_outer[:, None] * pos_half[None, :] % outer).astype(jnp.float32) / outer
    )
    inner_angle = (
        two_pi * (pos_inner[:, None] * pos_inner[None, :] % inner).astype(jnp.float32) / inner
    )
    twist_angle = (
        two_pi * (freq_outer[:, None] * pos_inner[None, :] % total).astype(jnp.float32) / total
    )
    return (
        jnp.cos(outer_angle),
        jnp.sin(outer_angle),
        jnp.cos(inner_angle),
        jnp.sin(inner_angle),
        jnp.cos(twist_angle),
        jnp.sin(twist_angle),
    )


def forward_dft(signal, tables):
    cos_outer, sin_outer, cos_inner, sin_inner, cos_twist, sin_twist = tables
    blocks = signal.reshape(signal.shape[0], cos_outer.shape[1], cos_inner.shape[0])
    real = jnp.einsum("kn,cnq->ckq", cos_outer, blocks, precision=highest)
    imag = -jnp.einsum("kn,cnq->ckq", sin_outer, blocks, precision=highest)
    turned_re = real * cos_twist + imag * sin_twist
    turned_im = imag * cos_twist - real * sin_twist
    out_re = jnp.einsum("ckq,qr->ckr", turned_re, cos_inner, precision=highest) + jnp.einsum(
        "ckq,qr->ckr", turned_im, sin_inner, precision=highest
    )
    out_im = jnp.einsum("ckq,qr->ckr", turned_im, cos_inner, precision=highest) - jnp.einsum(
        "ckq,qr->ckr", turned_re, sin_inner, precision=highest
    )
    return (out_re, out_im)


def inverse_dft(spec_re, spec_im, tables):
    cos_outer, sin_outer, cos_inner, sin_inner, cos_twist, sin_twist = tables
    total = cos_outer.shape[0] * cos_inner.shape[0]
    step_re = jnp.einsum("ckq,qr->ckr", spec_re, cos_inner, precision=highest) - jnp.einsum(
        "ckq,qr->ckr", spec_im, sin_inner, precision=highest
    )
    step_im = jnp.einsum("ckq,qr->ckr", spec_im, cos_inner, precision=highest) + jnp.einsum(
        "ckq,qr->ckr", spec_re, sin_inner, precision=highest
    )
    turned_re = step_re * cos_twist - step_im * sin_twist
    turned_im = step_im * cos_twist + step_re * sin_twist
    blocks = jnp.einsum("kn,ckq->cnq", cos_outer, turned_re, precision=highest) - jnp.einsum(
        "kn,ckq->cnq", sin_outer, turned_im, precision=highest
    )
    return (blocks / total).reshape(spec_re.shape[0], -1)


def on_device(block_input, norm_gain, short_taps, medium_taps, long_filter, grad_out):
    chans, tokens = block_input.shape
    seq_count = lax.axis_size("seq")
    med_count = medium_taps.shape[1]
    reach = med_count + short_taps.shape[1] - 2
    inputs32 = block_input.astype(jnp.float32)
    squares = lax.psum(jnp.sum(inputs32 * inputs32, axis=0), "ch")
    inv_rms = lax.rsqrt(squares / (chans * lax.axis_size("ch")) + 1e-05)
    normed = (inputs32 * inv_rms[None, :] * norm_gain[:, None]).astype(jnp.bfloat16)
    arrived, grad_chan = (
        lax.all_to_all(normed, "seq", split_axis=0, concat_axis=1, tiled=True),
        lax.all_to_all(grad_out, "seq", split_axis=0, concat_axis=1, tiled=True),
    )
    group, length = arrived.shape
    scale = length ** (-0.5)
    offset = lax.axis_index("seq") * group
    short_local = lax.dynamic_slice_in_dim(short_taps, offset, group, 0)
    medium_local = lax.dynamic_slice_in_dim(medium_taps, offset, group, 0)
    normed_pad = jnp.pad(arrived, ((0, 0), (reach, 0)))
    shorted_pad = depthwise(normed_pad, short_local[:, ::-1]).astype(jnp.bfloat16)
    filtered_chan = depthwise(shorted_pad, medium_local[:, ::-1]).astype(jnp.bfloat16)
    tables = fourier_tables(length)
    grad_re, grad_im = forward_dft(grad_chan.astype(jnp.float32), tables)
    filt_re, filt_im = forward_dft(long_filter, tables)
    sig_re, sig_im = forward_dft(filtered_chan.astype(jnp.float32), tables)
    grad_filtered = inverse_dft(
        filt_re * grad_re + filt_im * grad_im, filt_re * grad_im - filt_im * grad_re, tables
    ).astype(jnp.bfloat16)
    grad_long = (
        inverse_dft(
            sig_re * grad_re + sig_im * grad_im, sig_re * grad_im - sig_im * grad_re, tables
        )
        * scale
    )
    back_pad = jnp.pad(grad_filtered, ((0, 0), (0, reach)))
    shorted_grad = depthwise(back_pad, medium_local).astype(jnp.bfloat16)
    normed_grad = depthwise(shorted_grad, short_local).astype(jnp.bfloat16)
    medium_local_grad = depthwise(shorted_pad, grad_filtered)[:, ::-1] * scale
    short_local_grad = (
        depthwise(normed_pad[:, med_count - 1 :], shorted_grad[:, :length])[:, ::-1] * scale
    )
    leaving = normed_grad.reshape(group, seq_count, tokens)
    returned = lax.all_to_all(leaving, "seq", split_axis=1, concat_axis=0, tiled=True).reshape(
        chans, -1
    )
    return (returned, grad_long, medium_local_grad, short_local_grad)


def solution(mesh):
    placed = (
        P("ch", "seq"),
        P("ch"),
        P("ch", None),
        P("ch", None),
        P(("ch", "seq"), None),
        P("ch", "seq"),
    )
    return jax.shard_map(
        on_device,
        mesh=mesh,
        in_specs=placed,
        out_specs=(
            P("ch", "seq"),
            P(("ch", "seq"), None),
            P(("ch", "seq"), None),
            P(("ch", "seq"), None),
        ),
        check_vma=False,
    )
```

profile of v0, /device:TPU:0, one launch (start us, length us, event | category | flops | bytes accessed | tf_op | source)
XLA Modules:
  0.0 433.6 jit_solution(14907793232586408200)
XLA Ops:
  0.6 1.6 fusion.44
  2.2 8.4 %psum.7 = f32[256]{0:T(256)S(1)} all-reduce(f32[256]{0:T(256)S(1)} %fusion.44), channel_id=1, replica_groups=mesh['seq'=8,'ch'=4] {'ch'}, use_global_device_ids=true, to_apply=%region_1.0 | all-reduce | flops 256 | bytes 2048 | tf_op jit(solution)/shard_map/psum | solution.py:91
  10.6 1.6 fusion.46
  12.2 1.3 copy.122
  13.5 5.8 %all-to-all-start.2 = ((bf16[8,256,256]{1,2,0:T(8,128)(2,1)}), bf16[8,256,256]{1,2,0:T(8,128)(2,1)}, u32[]{:S(2)}, u32[]{:S(2)}) async-start(bf16[8,256,256]{1,2,0:T(8,128)(2,1)} %copy.122), calls=%async_computation.2 | async-start | bytes 2097152 | tf_op jit(solution)/shard_map/all_to_all | solution.py:95
  20.1 2.0 copy.147
  23.2 1.3 fusion.345
  24.6 5.1 %fusion.171 = f32[32,256,128]{2,0,1:T(8,128)} fusion(f32[256,16,128]{2,1,0:T(8,128)S(1)} %bitcast.202), kind=kOutput, calls=%fused_computation.179 | convolution fusion | flops 201333760 | bytes 6291456 | tf_op jit(solution)/shard_map/kn,cnq->ckq/dot_general | solution.py:55
  29.7 5.1 %fusion.163 = f32[32,256,128]{2,0,1:T(8,128)} fusion(f32[256,16,128]{2,1,0:T(8,128)S(1)} %bitcast.203), kind=kOutput, calls=%fused_computation.171 | convolution fusion | flops 201333760 | bytes 6291456 | tf_op jit(solution)/shard_map/kn,cnq->ckq/dot_general | solution.py:56
  34.9 9.3 %all-to-all-done.2 = bf16[8,256,256]{1,2,0:T(8,128)(2,1)} async-done(((bf16[8,256,256]{1,2,0:T(8,128)(2,1)}), bf16[8,256,256]{1,2,0:T(8,128)(2,1)}, u32[]{:S(2)}, u32[]{:S(2)}) %all-to-all-start.2) | async-done | bytes 1048608 | tf_op jit(solution)/shard_map/all_to_all | solution.py:95
  44.2 4.2 all-to-all-start
  48.4 1.5 pad_bitcast_fusion.1
  50.6 2.8 select_convert_fusion
  53.4 0.9 select_bitcast_fusion
  54.4 24.1 %fusion.66 = bf16[8,273,256]{2,0,1:T(8,128)(2,1)S(1)} fusion(bf16[256,1,128]{0,1,2:T(2,128)(2,1)S(1)} %copy.126, bf16[1,7,127,256]{3,1,2,0:T(8,128)(2,1)S(1)} %slice.20, bf16[1,8,273,256]{3,1,2,0:T(8,128)(2,1)S(1)} %select_bitcast_fusion), kind=kOutput, calls=%fused_computation.86 | convolution fusion | flops 148604928 | bytes 2757120 | tf_op jit(solution)/shard_map/conv_general_dilated | solution.py:12
  79.1 1.0 slice.21
  80.2 1.9 copy.142
  82.1 3.8 fusion.166
  85.9 3.9 fusion.158
  89.8 1.8 copy.106
  91.6 1.2 reshape.87
  92.8 3.2 fusion.161
  96.1 6.0 %add_bitcast_fusion = (f32[256,32,128]{2,1,0:T(8,128)S(1)}, f32[256,32,128]{2,1,0:T(8,128)S(1)}, f32[256,32,128]{2,1,0:T(8,128)S(1)}, f32[256,32,128]{2,1,0:T(8,128)S(1)}) fusion(f32[32,256,128]{2,0,1:T(8,128)S(1)} %fusion.161, f32[32,128]{1,0:T(8,128)S(1)} %get-tuple-element.38, f32[32,128]{1,0:T(8,128)S(1)} %get-tuple-element.39, ...), kind=kOutput, calls=%fused_computation.24 | convolution fusion | flops 216013824 | bytes 30441472 | tf_op jit(solution)/shard_map/kn,cnq->ckq/dot_general | solution.py:55
  102.1 8.6 %fusion.12 = f32[256,32,128]{2,0,1:T(8,128)} fusion(f32[256,32,128]{2,1,0:T(8,128)S(1)} %get-tuple-element.29), kind=kOutput, calls=%fused_computation.29 | convolution fusion | flops 1610842112 | bytes 8388608 | tf_op jit(solution)/shard_map/ckq,qr->ckr/dot_general | solution.py:59
  110.7 6.8 %fusion.10 = f32[256,32,128]{2,0,1:T(8,128)S(1)} fusion(f32[256,32,128]{2,1,0:T(8,128)S(1)} %get-tuple-element.29), kind=kOutput, calls=%fused_computation.27 | convolution fusion | flops 1610842112 | bytes 8388608 | tf_op jit(solution)/shard_map/ckq,qr->ckr/dot_general | solution.py:62
  117.5 7.2 %fusion.18 = f32[256,32,128]{2,0,1:T(8,128)S(1)} fusion(f32[256,32,128]{2,1,0:T(8,128)S(1)} %get-tuple-element.36), kind=kOutput, calls=%fused_computation.35 | convolution fusion | flops 1610842112 | bytes 8388608 | tf_op jit(solution)/shard_map/ckq,qr->ckr/dot_general | solution.py:62
  124.7 7.1 %fusion.20 = f32[256,32,128]{2,0,1:T(8,128)S(1)} fusion(f32[256,32,128]{2,1,0:T(8,128)S(1)} %get-tuple-element.36), kind=kOutput, calls=%fused_computation.37 | convolution fusion | flops 1610842112 | bytes 8388608 | tf_op jit(solution)/shard_map/ckq,qr->ckr/dot_general | solution.py:59
  131.8 13.2 %fusion.92 = f32[256,32,128]{2,0,1:T(8,128)} fusion(f32[256,128,32]{1,2,0:T(8,128)S(1)} %copy-done.2, f32[256,128,32]{1,2,0:T(8,128)S(1)} %copy-done.3, f32[32,128]{1,0:T(8,128)S(1)} %get-tuple-element.38, f32[32,128]{1,0:T(8,128)S(1)} %get-tuple-element.39), kind=kOutput, calls=%fused_computation.109 | convolution fusion | flops 1615036416 | bytes 12615680 | tf_op jit(solution)/shard_map/ckq,qr->ckr/dot_general | solution.py:59
  145.0 12.9 %fusion.88 = f32[256,32,128]{2,0,1:T(8,128)} fusion(f32[256,128,32]{1,2,0:T(8,128)S(1)} %copy-done.2, f32[256,128,32]{1,2,0:T(8,128)S(1)} %copy-done.3, f32[32,128]{1,0:T(8,128)S(1)} %get-tuple-element.38, f32[32,128]{1,0:T(8,128)S(1)} %get-tuple-element.39), kind=kOutput, calls=%fused_computation.108 | convolution fusion | flops 1615036416 | bytes 12615680 | tf_op jit(solution)/shard_map/ckq,qr->ckr/dot_general | solution.py:62
  158.0 1.2 copy.133
  159.2 14.5 %convolution_add_fusion.1 = f32[256,32,128]{2,0,1:T(8,128)} fusion(f32[256,32,128]{2,0,1:T(8,128)} %fusion.92, f32[256,128,32]{1,2,0:T(8,128)S(1)} %copy-done.2, f32[256,128,32]{1,2,0:T(8,128)S(1)} %copy-done.3, f32[32,128]{1,0:T(8,128)S(1)} %get-tuple-element.38, f32[32,128]{1,0:T(8,128)S(1)} %get-tuple-element.39), kind=kOutput, calls=%fused_computation.62 | convolution fusion | flops 1616084992 | bytes 16809984 | tf_op jit(solution)/shard_map/ckq,qr->ckr/dot_general | solution.py:59
  173.7 8.4 %fusion.36 = f32[256,32,128]{2,0,1:T(8,128)} fusion(f32[256,32,128]{2,0,1:T(8,128)S(1)} %copy-done.8, f32[256,32,128]{2,1,0:T(8,128)S(1)} %get-tuple-element.28), kind=kOutput, calls=%fused_computation.57 | convolution fusion | flops 1611890688 | bytes 12582912 | tf_op jit(solution)/shard_map/ckq,qr->ckr/dot_general | solution.py:59
  182.1 8.6 %fusion.39 = f32[256,32,128]{2,0,1:T(8,128)} fusion(f32[256,32,128]{2,0,1:T(8,128)S(1)} %fusion.10, f32[256,32,128]{2,1,0:T(8,128)S(1)} %get-tuple-element.28), kind=kOutput, calls=%fused_computation.58 | convolution fusion | flops 1611890688 | bytes 12582912 | tf_op jit(solution)/shard_map/ckq,qr->ckr/dot_general | solution.py:62
  190.7 8.6 %fusion.33 = f32[256,32,128]{2,0,1:T(8,128)} fusion(f32[256,32,128]{2,0,1:T(8,128)S(1)} %fusion.18, f32[256,32,128]{2,1,0:T(8,128)S(1)} %get-tuple-element.37), kind=kOutput, calls=%fused_computation.56 | convolution fusion | flops 1611890688 | bytes 12582912 | tf_op jit(solution)/shard_map/ckq,qr->ckr/dot_general | solution.py:62
  199.3 8.4 %fusion.30 = f32[256,32,128]{2,0,1:T(8,128)} fusion(f32[256,32,128]{2,0,1:T(8,128)S(1)} %fusion.20, f32[256,32,128]{2,1,0:T(8,128)S(1)} %get-tuple-element.37), kind=kOutput, calls=%fused_computation.55 | convolution fusion | flops 1611890688 | bytes 12582912 | tf_op jit(solution)/shard_map/ckq,qr->ckr/dot_general | solution.py:59
  207.7 22.7 %multiply_subtract_fusion.1 = (f32[256,32,128]{2,0,1:T(8,128)}, f32[256,32,128]{2,0,1:T(8,128)}, f32[256,32,128]{2,0,1:T(8,128)}, f32[256,32,128]{2,0,1:T(8,128)}) fusion(f32[256,32,128]{2,0,1:T(8,128)} %fusion.36, f32[256,32,128]{2,0,1:T(8,128)} %convolution_add_fusion.1, f32[256,32,128]{2,0,1:T(8,128)} %fusion.39, f32[256,32,128]{2,0,1:T(8,128)} %fusion.33, ...), kind=kOutput, calls=%fused_computation.17 | convolution fusion | flops 1628667904 | bytes 50364416 | tf_op jit(solution)/shard_map/ckq,qr->ckr/dot_general | solution.py:62
  230.4 6.0 %fusion.111 = f32[256,32,128]{2,0,1:T(8,128)S(1)} fusion(f32[256,32,128]{2,0,1:T(8,128)} %get-tuple-element.21), kind=kOutput, calls=%fused_computation.131 | convolution fusion | flops 1610842112 | bytes 8388608 | tf_op jit(solution)/shard_map/ckq,qr->ckr/dot_general | solution.py:71
  236.5 5.6 %fusion.109 = f32[256,32,128]{2,0,1:T(8,128)} fusion(f32[256,32,128]{2,0,1:T(8,128)S(1)} %copy-done.6), kind=kOutput, calls=%fused_computation.129 | convolution fusion | flops 1610842112 | bytes 8388608 | tf_op jit(solution)/shard_map/ckq,qr->ckr/dot_general | solution.py:74
  242.1 3.8 convolution_subtract_fusion
  245.9 3.8 fusion.117
  249.7 3.8 fusion.115
  253.5 4.2 convolution_subtract_fusion.2
  257.7 5.5 %convolution_add_fusion.2 = f32[256,32,128]{2,0,1:T(8,128)} fusion(f32[256,32,128]{2,0,1:T(8,128)S(1)} %fusion.115, f32[256,32,128]{2,0,1:T(8,128)S(1)} %copy-done.4), kind=kOutput, calls=%fused_computation.63 | convolution fusion | flops 1611890688 | bytes 12582912 | tf_op jit(solution)/shard_map/ckq,qr->ckr/dot_general | solution.py:74
  263.3 11.6 %multiply_subtract_fusion = (f32[256,32,128]{2,0,1:T(8,128)}, f32[256,32,128]{2,0,1:T(8,128)}, f32[256,32,128]{2,0,1:T(8,128)}, f32[256,32,128]{2,0,1:T(8,128)}) fusion(f32[256,32,128]{2,0,1:T(8,128)S(1)} %convolution_subtract_fusion, f32[32,128]{1,0:T(8,128)S(1)} %get-tuple-element.38, f32[32,128]{1,0:T(8,128)S(1)} %get-tuple-element.39, ...), kind=kOutput, calls=%fused_computation.16 | convolution fusion | flops 1624473600 | bytes 37781504 | tf_op jit(solution)/shard_map/ckq,qr->ckr/dot_general | solution.py:74
  274.9 7.0 %fusion.6 = f32[256,128,16]{1,2,0:T(8,128)S(1)} fusion(f32[256,32,128]{2,0,1:T(8,128)} %get-tuple-element.34), kind=kOutput, calls=%fused_computation.11 | convolution fusion | flops 201333760 | bytes 6291456 | tf_op jit(solution)/shard_map/kn,ckq->cnq/dot_general | solution.py:79
  281.9 4.9 %fusion.69 = bf16[256,16,128]{2,1,0:T(8,128)(2,1)S(1)} fusion(f32[256,128,16]{1,2,0:T(8,128)S(1)} %fusion.6, f32[256,32,128]{2,0,1:T(8,128)S(1)} %copy-done.10), kind=kOutput, calls=%fused_computation.88 | convolution fusion | flops 202906624 | bytes 7340032 | tf_op jit(solution)/shard_map/kn,ckq->cnq/dot_general | solution.py:79
  287.6 1.3 convert_element_type.181
  289.9 28.6 %select_convert_fusion.1 = bf16[8,273,256]{2,0,1:T(8,128)(2,1)S(1)} fusion(bf16[256,1,128]{0,1,2:T(2,128)(2,1)S(1)} %copy-done.14, bf16[256,1,7,127]{0,2,3,1:T(8,128)(2,1)S(1)} %slice.16, bf16[256,1,8,273]{0,2,3,1:T(8,128)(2,1)S(1)} %copy.117, pred[8,273]{0,1:T(8,128)(4,1)S(1)} %copy-done.15), kind=kOutput, calls=%fused_computation.54 | convolution fusion | flops 149164032 | bytes 2759304 | tf_op jit(solution)/shard_map/conv_general_dilated | solution.py:12
  318.5 0.9 select_bitcast_fusion.1
  319.4 1.2 copy.136
  320.7 2.4 convolution_convert_fusion
  323.7 1.0 slice.18
  324.7 5.9 %all-to-all-start.1 = ((bf16[256,8,256]{0,2,1:T(8,128)(2,1)}), bf16[256,8,256]{0,2,1:T(8,128)(2,1)}, u32[]{:S(2)}, u32[]{:S(2)}) async-start(bf16[256,8,256]{0,2,1:T(8,128)(2,1)} %bitcast.19), calls=%async_computation.1 | async-start | bytes 2097152 | tf_op jit(solution)/shard_map/all_to_all | solution.py:127
  330.6 6.8 %fusion.2 = f32[256,128,16]{1,2,0:T(8,128)S(1)} fusion(f32[256,32,128]{2,0,1:T(8,128)} %get-tuple-element.25), kind=kOutput, calls=%fused_computation.6 | convolution fusion | flops 201333760 | bytes 6291456 | tf_op jit(solution)/shard_map/kn,ckq->cnq/dot_general | solution.py:79
  337.5 6.5 %reshape.129 = bf16[1,2184,256]{2,0,1:T(2,128)(2,1)} reshape(bf16[8,273,256]{2,1,0:T(8,128)(2,1)} %copy.133) | data formatting | bytes 2236416 | tf_op jit(solution)/shard_map/convert_element_type | solution.py:104
  343.9 5.9 %copy.135 = bf16[256,1,2048]{0,1,2:T(2,128)(2,1)} copy(bf16[256,1,2048]{2,0,1:T(8,128)(2,1)} %convert_element_type.181) | data formatting | bytes 2097152 | tf_op jit(solution)/shard_map/convert_element_type | solution.py:112
  349.9 25.4 %fusion.326 = f32[1,256,128]{1,0,2:T(1,128)S(1)} fusion(bf16[1,2184,256]{2,0,1:T(2,128)(2,1)} %reshape.129, bf16[256,1,2048]{0,1,2:T(2,128)(2,1)} %copy.135), kind=kOutput, calls=%fused_computation.326 | convolution fusion | flops 134217728 | bytes 2297856 | tf_op jit(solution)/shard_map/conv_general_dilated | solution.py:12
  375.4 2.6 reshape.95
  378.0 2.3 slice_bitcast_fusion
  380.3 6.9 %subtract_multiply_fusion = f32[256,128,16]{1,2,0:T(8,128)S(1)} fusion(f32[256,128,16]{1,2,0:T(8,128)S(1)} %fusion.2, f32[256,32,128]{2,0,1:T(8,128)} %get-tuple-element.24), kind=kOutput, calls=%fused_computation.72 | convolution fusion | flops 202382336 | bytes 8388608 | tf_op jit(solution)/shard_map/kn,ckq->cnq/dot_general | solution.py:79
  387.2 2.2 copy.217
  390.2 1.5 slice_bitcast_fusion.1
  391.8 38.4 %fusion.42 = f32[1,256,7]{1,0,2:T(1,128)S(1)} fusion(bf16[1,256,2054]{1,2,0:T(8,128)(2,1)S(1)} %slice_bitcast_fusion.1, bf16[256,1,2048]{0,2,1:T(8,128)(2,1)S(1)} %slice_bitcast_fusion.2), kind=kOutput, calls=%fused_computation.65 | convolution fusion | flops 7340032 | bytes 2107392 | tf_op jit(solution)/shard_map/conv_general_dilated | solution.py:12
  430.9 2.3 copy.121
  (71 shorter events, 7.3 us)
Async XLA Ops:
  0.6 18.7 %copy-start = (bf16[2048,128]{1,0:T(8,128)(2,1)S(1)}, bf16[2048,128]{1,0:T(8,128)(2,1)}, u32[]{:S(2)}) copy-start(bf16[2048,128]{1,0:T(8,128)(2,1)} %param.9) | copy-start | bytes 1572868
  13.5 30.7 %all-to-all-start.2 = ((bf16[8,256,256]{1,2,0:T(8,128)(2,1)}), bf16[8,256,256]{1,2,0:T(8,128)(2,1)}, u32[]{:S(2)}, u32[]{:S(2)}) async-start(bf16[8,256,256]{1,2,0:T(8,128)(2,1)} %copy.122), calls=%async_computation.2 | async-start | bytes 2097152 | tf_op jit(solution)/shard_map/all_to_all | solution.py:95
  44.2 45.7 %all-to-all-start = ((bf16[8,256,256]{2,1,0:T(8,128)(2,1)}), bf16[8,256,256]{2,1,0:T(8,128)(2,1)}, u32[]{:S(2)}, u32[]{:S(2)}) async-start(bf16[8,256,256]{2,1,0:T(8,128)(2,1)} %bitcast.210), calls=%async_computation | async-start | bytes 2097152 | tf_op jit(solution)/shard_map/all_to_all | solution.py:96
  48.4 2.2 copy-start.16
  53.4 25.2 %copy-start.11 = (bf16[8,273,256]{2,0,1:T(8,128)(2,1)}, bf16[8,273,256]{2,0,1:T(8,128)(2,1)S(1)}, u32[]{:S(2)}) copy-start(bf16[8,273,256]{2,0,1:T(8,128)(2,1)S(1)} %select_convert_fusion) | copy-start | bytes 3354628
  92.8 3.3 copy-start.9
  124.7 7.1 %copy-start.2 = (f32[256,128,32]{1,2,0:T(8,128)S(1)}, f32[256,128,32]{1,2,0:T(8,128)}, u32[]{:S(2)}) copy-start(f32[256,128,32]{1,2,0:T(8,128)} %fusion.166) | copy-start | bytes 12582916
  124.7 7.1 %copy-start.3 = (f32[256,128,32]{1,2,0:T(8,128)S(1)}, f32[256,128,32]{1,2,0:T(8,128)}, u32[]{:S(2)}) copy-start(f32[256,128,32]{1,2,0:T(8,128)} %fusion.158) | copy-start | bytes 12582916
  145.0 12.9 %copy-start.12 = (bf16[8,273,256]{2,0,1:T(8,128)(2,1)S(1)}, bf16[8,273,256]{2,0,1:T(8,128)(2,1)}, u32[]{:S(2)}) copy-start(bf16[8,273,256]{2,0,1:T(8,128)(2,1)} %copy-done.11) | copy-start | bytes 3354628
  159.2 14.5 %copy-start.8 = (f32[256,32,128]{2,0,1:T(8,128)S(1)}, f32[256,32,128]{2,0,1:T(8,128)}, u32[]{:S(2)}) copy-start(f32[256,32,128]{2,0,1:T(8,128)} %fusion.12) | copy-start | bytes 12582916
  230.4 6.0 %copy-start.6 = (f32[256,32,128]{2,0,1:T(8,128)S(1)}, f32[256,32,128]{2,0,1:T(8,128)}, u32[]{:S(2)}) copy-start(f32[256,32,128]{2,0,1:T(8,128)} %get-tuple-element.20) | copy-start | bytes 12582916
  242.1 3.8 copy-start.4
  245.9 3.8 copy-start.5
  257.7 5.6 %copy-start.7 = (f32[256,32,128]{2,0,1:T(8,128)S(1)}, f32[256,32,128]{2,0,1:T(8,128)}, u32[]{:S(2)}) copy-start(f32[256,32,128]{2,0,1:T(8,128)} %get-tuple-element.21) | copy-start | bytes 12582916
  274.9 7.0 %copy-start.10 = (f32[256,32,128]{2,0,1:T(8,128)S(1)}, f32[256,32,128]{2,0,1:T(8,128)}, u32[]{:S(2)}) copy-start(f32[256,32,128]{2,0,1:T(8,128)} %get-tuple-element.35) | copy-start | bytes 12582916
  289.0 0.9 copy-start.14
  289.0 0.9 copy-start.15
  318.5 2.2 copy-start.17
  324.7 106.2 %all-to-all-start.1 = ((bf16[256,8,256]{0,2,1:T(8,128)(2,1)}), bf16[256,8,256]{0,2,1:T(8,128)(2,1)}, u32[]{:S(2)}, u32[]{:S(2)}) async-start(bf16[256,8,256]{0,2,1:T(8,128)(2,1)} %bitcast.19), calls=%async_computation.1 | async-start | bytes 2097152 | tf_op jit(solution)/shard_map/all_to_all | solution.py:127
  387.2 4.5 %copy-start.13 = (bf16[256,2054]{0,1:T(8,128)(2,1)S(1)}, bf16[256,2054]{0,1:T(8,128)(2,1)}, u32[]{:S(2)}) copy-start(bf16[256,2054]{0,1:T(8,128)(2,1)} %slice_bitcast_fusion) | copy-start | bytes 3154948
  391.8 41.4 %copy-start.1 = (bf16[2048,128]{1,0:T(8,128)(2,1)S(1)}, bf16[2048,128]{1,0:T(8,128)(2,1)}, u32[]{:S(2)}) copy-start(bf16[2048,128]{1,0:T(8,128)(2,1)} %param.9) | copy-start | bytes 1572868
where the time goes:
time: 440 us; the launch traced here: 434 us
  matrix products  346 us (79%)
  local copies, waits for them, and re-layouts  46.6 us (11%)
  starting transfers between devices  15.9 us (4%)
  waiting for transfers between devices  9.3 us (2%)
  blocking collectives  8.36 us (2%)
  other arithmetic  5.68 us (1%)
    conv_general_dilated x6, matrix products, depthwise(): lax.conv_general_dilated(signal[None], taps[:, None, :], (1,), 'VALID', d...  122 us
    dot_general x3, matrix products, forward_dft(): jnp.einsum('ckq,qr->ckr', turned_re, sin_inner, precision=highest)  39.9 us
    dot_general x3, matrix products, forward_dft(): jnp.einsum('ckq,qr->ckr', turned_im, sin_inner, precision=highest)  30.2 us
    dot_general x3, matrix products, forward_dft(): jnp.einsum('ckq,qr->ckr', turned_re, cos_inner, precision=highest)  30 us
    dot_general x3, matrix products, forward_dft(): jnp.einsum('ckq,qr->ckr', turned_im, cos_inner, precision=highest)  26.9 us
    dot_general x2, matrix products, inverse_dft(): jnp.einsum('ckq,qr->ckr', spec_re, sin_inner, precision=highest)  17.2 us
    dot_general x3, matrix products, forward_dft(): real = jnp.einsum('kn,cnq->ckq', cos_outer, blocks, precision=highest)  15 us
    dot_general x2, matrix products, inverse_dft(): jnp.einsum('kn,ckq->cnq', sin_outer, turned_im, precision=highest)  13.8 us
  transfers between devices with their start and end apart: 3, of which 1 were waited for; matrix products, arithmetic and copies ran while one was open for 36% of the time, Pallas kernels for 0%

commit v1 on v0

v1 whole, which is shorter than its diff:
```python
import functools
import math

import jax
import jax.numpy as jnp
import ml_dtypes
import numpy as np
from jax import lax
from jax.experimental import pallas as pl
from jax.experimental.pallas import tpu as pltpu
from jax.sharding import PartitionSpec as P

LANES = 128
ROWS = 16
CHUNKS = 1


def halves(table):
    high = table.astype(np.float32).astype(ml_dtypes.bfloat16)
    low = (table - high.astype(np.float64)).astype(np.float32).astype(ml_dtypes.bfloat16)
    return high, low


@functools.lru_cache(maxsize=None)
def tables(blocks):
    outer = blocks + 1
    k = np.arange(outer)[:, None]
    a = np.arange(blocks)[None, :]
    q = np.arange(LANES)
    angle = 2.0 * math.pi * ((4 * k + 1) * a % (4 * outer)) / (4.0 * outer)
    eye = np.eye(ROWS)
    split = np.stack([np.cos(angle), -np.sin(angle)])
    ahead = np.einsum("xka,cd->xkcad", split, eye)
    ahead = ahead.reshape(2 * outer * ROWS, blocks * ROWS)
    back = ahead.T
    twist = 2.0 * math.pi * (4 * k + 1) * q[None, :] / (4.0 * outer * LANES)
    twist_re = np.repeat(np.cos(twist), ROWS, axis=0).astype(np.float32)
    twist_im = np.repeat(-np.sin(twist), ROWS, axis=0).astype(np.float32)
    inner = 2.0 * math.pi * (q[:, None] * q[None, :] % LANES) / LANES
    cos, sin = np.cos(inner), np.sin(inner)
    turn = np.block([[cos, -sin], [sin, cos]])
    return (
        *halves(ahead),
        *halves(back),
        twist_re,
        twist_im,
        *halves(turn),
        *halves(turn.T),
    )


def times(a, b):
    return (a[0] * b[0] - a[1] * b[1], a[0] * b[1] + a[1] * b[0])


def times_conj(a, b):
    return (a[0] * b[0] + a[1] * b[1], a[1] * b[0] - a[0] * b[1])


def dot(a, b):
    return jnp.dot(a, b, preferred_element_type=jnp.float32)


def parted(value):
    high = value.astype(jnp.bfloat16)
    return high, (value - high.astype(jnp.float32)).astype(jnp.bfloat16)


def spectral_kernel(
    blocks,
    x_ref,
    g_ref,
    h_ref,
    inv_ref,
    gain_ref,
    short_ref,
    medium_ref,
    ahead_hi,
    ahead_lo,
    back_hi,
    back_lo,
    twist_re,
    twist_im,
    turn_hi,
    turn_lo,
    turn_back_hi,
    turn_back_lo,
    normed_out,
    long_out,
    medium_out,
    short_out,
    first,
    last_hi,
    last_lo,
):
    outer = blocks + 1
    groups = x_ref.shape[1] // ROWS
    per = x_ref.shape[2] // LANES
    half = outer * ROWS
    scale = 1.0 / (outer * LANES)
    root = (blocks * LANES) ** (-0.5)

    def piece(ref, group, block):
        lanes = slice((block % per) * LANES, (block % per + 1) * LANES)
        return ref[block // per, group * ROWS : (group + 1) * ROWS, lanes]

    def normed_piece(group, block):
        raw = piece(x_ref, group, block).astype(jnp.float32)
        inv = inv_ref[:, block * LANES : (block + 1) * LANES]
        gain = gain_ref[group * ROWS : (group + 1) * ROWS, :]
        return (raw * inv * gain).astype(jnp.bfloat16)

    for group in range(groups):
        lanes = slice(group * LANES, (group + 1) * LANES)
        rows = slice(group * ROWS, (group + 1) * ROWS)
        normed = jnp.concatenate([normed_piece(group, b) for b in range(blocks)], axis=0)
        grads = jnp.concatenate([piece(g_ref, group, b) for b in range(blocks)], axis=0)
        taps = jnp.concatenate(
            [h_ref[rows, b * LANES : (b + 1) * LANES] for b in range(blocks)], axis=0
        )
        taps_hi, taps_lo = parted(taps)
        pair = jnp.concatenate([normed, grads], axis=1)
        both = dot(ahead_hi[...], pair) + dot(ahead_lo[...], pair)
        first[0, :, lanes] = both[:, :LANES]
        first[1, :, lanes] = both[:, LANES:]
        pair = jnp.concatenate([taps_hi, taps_lo], axis=1)
        both = dot(ahead_hi[...], pair)
        first[2, :, lanes] = both[:, :LANES] + both[:, LANES:] + dot(ahead_lo[...], taps_hi)

    def at_freq(k, sums):
        top = pl.multiple_of(k * ROWS, ROWS)
        bottom = pl.multiple_of(half + k * ROWS, ROWS)
        t_re = twist_re[pl.ds(top, ROWS), :]
        t_im = twist_im[pl.ds(top, ROWS), :]
        stack = []
        for signal in range(3):
            for group in range(groups):
                lanes = slice(group * LANES, (group + 1) * LANES)
                value = (
                    first[signal, pl.ds(top, ROWS), lanes],
                    first[signal, pl.ds(bottom, ROWS), lanes],
                )
                stack.append(jnp.concatenate(times(value, (t_re, t_im)), axis=1))
        for ref in (short_ref, medium_ref):
            for group in range(groups):
                taps = ref[group * ROWS : (group + 1) * ROWS, :].astype(jnp.float32)
                stack.append(jnp.concatenate([taps * t_re, taps * t_im], axis=1))
        high, low = parted(jnp.concatenate(stack, axis=0))
        spec = dot(high, turn_hi[...]) + dot(low, turn_hi[...]) + dot(high, turn_lo[...])
        count = groups * ROWS
        normed, grads, taps, short, medium = [
            (spec[i * count : (i + 1) * count, :LANES], spec[i * count : (i + 1) * count, LANES:])
            for i in range(5)
        ]
        shorted = times(short, normed)
        grad_long = times_conj(grads, times(medium, shorted))
        grad_filtered = times_conj(grads, taps)
        grad_medium = times_conj(grad_filtered, shorted)
        grad_shorted = times_conj(grad_filtered, medium)
        grad_short = times_conj(grad_shorted, normed)
        grad_normed = times_conj(grad_shorted, short)
        stack = [
            jnp.concatenate(value, axis=1)
            for value in (grad_normed, grad_long, grad_medium, grad_short)
        ]
        high, low = parted(jnp.concatenate(stack, axis=0))
        step = (
            dot(high, turn_back_hi[...])
            + dot(low, turn_back_hi[...])
            + dot(high, turn_back_lo[...])
        )
        for signal in range(2):
            for group in range(groups):
                at = signal * count + group * ROWS
                lanes = slice(group * LANES, (group + 1) * LANES)
                value = (step[at : at + ROWS, :LANES], step[at : at + ROWS, LANES:])
                turned = times_conj(value, (t_re, t_im))
                for where, part in zip((top, bottom), turned):
                    part_hi, part_lo = parted(part)
                    last_hi[signal, pl.ds(where, ROWS), lanes] = part_hi
                    last_lo[signal, pl.ds(where, ROWS), lanes] = part_lo
        result = []
        for signal in range(2):
            for group in range(groups):
                at = (2 + signal) * count + group * ROWS
                real = step[at : at + ROWS, :LANES] * t_re + step[at : at + ROWS, LANES:] * t_im
                result.append(sums[signal * groups + group] + real)
        return tuple(result)

    zero = jnp.zeros((ROWS, LANES), jnp.float32)
    sums = lax.fori_loop(0, outer, at_freq, (zero,) * (2 * groups))
    for group in range(groups):
        rows = slice(group * ROWS, (group + 1) * ROWS)
        medium_out[rows, :] = sums[group] * (scale * root)
        short_out[rows, :] = sums[groups + group] * (scale * root)
    for signal in range(2):
        value = (
            dot(back_hi[...], last_hi[signal])
            + dot(back_hi[...], last_lo[signal])
            + dot(back_lo[...], last_hi[signal])
        )
        for group in range(groups):
            rows = slice(group * ROWS, (group + 1) * ROWS)
            for block in range(blocks):
                part = value[
                    block * ROWS : (block + 1) * ROWS, group * LANES : (group + 1) * LANES
                ]
                lanes = slice((block % per) * LANES, (block % per + 1) * LANES)
                if signal == 0:
                    normed_out[block // per, rows, lanes] = (part * scale).astype(jnp.bfloat16)
                else:
                    long_out[rows, block * LANES : (block + 1) * LANES] = part * (scale * root)


def spectral(x, g, h, inv, gain, short, medium, interpret=False):
    owners, chans, tokens = x.shape
    length = owners * tokens
    blocks = length // LANES
    outer = blocks + 1
    size = min(chans, 64 if blocks <= 16 else ROWS)
    consts = [jnp.asarray(t) for t in tables(blocks)]
    whole = pl.BlockSpec(memory_space=pltpu.VMEM)
    cut = pl.BlockSpec((owners, size, tokens), lambda i: (0, i, 0))

    def rows(width):
        return pl.BlockSpec((size, width), lambda i: (i, 0))

    lanes = size // ROWS * LANES
    return pl.pallas_call(
        functools.partial(spectral_kernel, blocks),
        grid=(chans // size,),
        in_specs=[
            cut,
            cut,
            rows(length),
            pl.BlockSpec((1, length), lambda i: (0, 0)),
            rows(1),
            rows(LANES),
            rows(LANES),
        ]
        + [whole] * len(consts),
        out_specs=[cut, rows(length), rows(LANES), rows(LANES)],
        out_shape=[
            jax.ShapeDtypeStruct((owners, chans, tokens), jnp.bfloat16),
            jax.ShapeDtypeStruct((chans, length), jnp.float32),
            jax.ShapeDtypeStruct((chans, LANES), jnp.float32),
            jax.ShapeDtypeStruct((chans, LANES), jnp.float32),
        ],
        scratch_shapes=[
            pltpu.VMEM((3, 2 * outer * ROWS, lanes), jnp.float32),
            pltpu.VMEM((2, 2 * outer * ROWS, lanes), jnp.bfloat16),
            pltpu.VMEM((2, 2 * outer * ROWS, lanes), jnp.bfloat16),
        ],
        compiler_params=pltpu.CompilerParams(vmem_limit_bytes=56 * 1024 * 1024),
        interpret=interpret,
    )(x, g, h, inv, gain, short, medium, *consts)


def on_device(block_input, norm_gain, short_taps, medium_taps, long_filter, grad_out, interpret=False):
    chans, tokens = block_input.shape
    seq_count = lax.axis_size("seq")
    ch_count = lax.axis_size("ch")
    group = chans // seq_count
    length = seq_count * tokens
    short_count = short_taps.shape[1]
    inputs32 = block_input.astype(jnp.float32)
    squares = jnp.sum(inputs32 * inputs32, axis=0)
    everyones = lax.all_gather(squares, ("ch", "seq")).reshape(ch_count, length)
    inv_rms = lax.rsqrt(jnp.sum(everyones, axis=0) / (chans * ch_count) + 1e-05)[None, :]
    offset = lax.axis_index("seq") * group
    gain = lax.dynamic_slice_in_dim(norm_gain, offset, group, 0)[:, None]
    short = lax.dynamic_slice_in_dim(short_taps, offset, group, 0)
    short = jnp.pad(short, ((0, 0), (0, LANES - short_count)))
    medium = lax.dynamic_slice_in_dim(medium_taps, offset, group, 0)
    chunks = CHUNKS if group % (CHUNKS * ROWS) == 0 else 1
    part = group // chunks
    x_all = block_input.reshape(seq_count, group, tokens)
    g_all = grad_out.reshape(seq_count, group, tokens)
    results = []
    for chunk in range(chunks):
        at = slice(chunk * part, (chunk + 1) * part)
        x = lax.all_to_all(x_all[:, at], "seq", split_axis=0, concat_axis=0, tiled=True)
        g = lax.all_to_all(g_all[:, at], "seq", split_axis=0, concat_axis=0, tiled=True)
        normed, long, med, sho = spectral(
            x, g, long_filter[at], inv_rms, gain[at], short[at], medium[at], interpret
        )
        normed = lax.all_to_all(normed, "seq", split_axis=0, concat_axis=0, tiled=True)
        results.append((normed, long, med, sho[:, :short_count]))
    if chunks == 1:
        normed, long, med, sho = results[0]
    else:
        normed = jnp.concatenate([r[0] for r in results], axis=1)
        long, med, sho = [jnp.concatenate([r[i] for r in results], axis=0) for i in (1, 2, 3)]
    return (normed.reshape(chans, tokens), long, med[:, : medium_taps.shape[1]], sho)


def solution(mesh):
    placed = (
        P("ch", "seq"),
        P("ch"),
        P("ch", None),
        P("ch", None),
        P(("ch", "seq"), None),
        P("ch", "seq"),
    )
    return jax.shard_map(
        on_device,
        mesh=mesh,
        in_specs=placed,
        out_specs=(
            P("ch", "seq"),
            P(("ch", "seq"), None),
            P(("ch", "seq"), None),
            P(("ch", "seq"), None),
        ),
        check_vma=False,
    )
```

time: 440 us -> 216 us (0.49); the launches traced: 434 us -> 216 us
  matrix products: 346 us -> 0 us
  blocking collectives: 8.36 us -> 112 us
  Pallas kernels: 0 us -> 63.7 us
  local copies, waits for them, and re-layouts: 46.6 us -> 6.3 us
  waiting for transfers between devices: 9.3 us -> 23.1 us
  starting transfers between devices: 15.9 us -> 7.29 us
    dot_general x30 -> x0, matrix products: 224 us -> none  [the longest x3 39.9 us: forward_dft(): jnp.einsum('ckq,qr->ckr', turned_re, sin_inner, precision=highest)]
    conv_general_dilated x6 -> x0, matrix products: 122 us -> none  [depthwise(): lax.conv_general_dilated(signal[None], taps[:, None, :], (1,), 'VALID', d...]
    all_gather x0 -> x1, blocking collectives: none -> 79.2 us  [on_device(): everyones = lax.all_gather(squares, ('ch', 'seq')).reshape(ch_count, length)]
    pallas_call x0 -> x1, Pallas kernels: none -> 63.7 us  [spectral(): pl.pallas_call(functools.partial(spectral_kernel, blocks), grid=(chans //...]
    all_to_all x0 -> x1, blocking collectives: none -> 33.3 us  [on_device(): lax.all_to_all(g_all[:, at], 'seq', split_axis=0, concat_axis=0, tiled=True)]
    convert_element_type x17 -> x0, local copies, waits for them, and re-layouts: 27.1 us -> none  [the longest x3 8.02 us: on_device(): grad_filtered = inverse_dft(filt_re * grad_re + filt_im * grad_im, filt_r...]
    all_to_all x3 -> x2, waiting for transfers between devices: 9.3 us -> 23.1 us  [the longest x1 23.1 us: on_device(): lax.all_to_all(normed, 'seq', split_axis=0, concat_axis=0, tiled=True)]
    all_to_all x3 -> x2, starting transfers between devices: 15.9 us -> 7.29 us  [the longest x1 3.7 us: on_device(): lax.all_to_all(normed, 'seq', split_axis=0, concat_axis=0, tiled=True)]
  transfers between devices with their start and end apart: 3 -> 2, of which waited for: 1 -> 1; matrix products, arithmetic and copies ran while one was open for 36% -> 3% of each run, Pallas kernels for 0% -> 0%
where the time goes in v1:
time: 216 us
  blocking collectives  112 us (52%)
  Pallas kernels  63.7 us (29%)
  waiting for transfers between devices  23.1 us (11%)
  starting transfers between devices  7.29 us (3%)
  local copies, waits for them, and re-layouts  6.3 us (3%)
  other arithmetic  2.27 us (1%)
    all_gather x1, blocking collectives, on_device(): everyones = lax.all_gather(squares, ('ch', 'seq')).reshape(ch_count, length)  79.2 us
    pallas_call x1, Pallas kernels, spectral(): pl.pallas_call(functools.partial(spectral_kernel, blocks), grid=(chans //...  63.7 us
    all_to_all x1, blocking collectives, on_device(): lax.all_to_all(g_all[:, at], 'seq', split_axis=0, concat_axis=0, tiled=True)  33.3 us
    all_to_all x1, waiting for transfers between devices, on_device(): lax.all_to_all(normed, 'seq', split_axis=0, concat_axis=0, tiled=True)  23.1 us
  transfers between devices with their start and end apart: 2, of which 1 were waited for; matrix products, arithmetic and copies ran while one was open for 3% of the time, Pallas kernels for 0%

profile of v1, /device:TPU:0, one launch (start us, length us, event | category | flops | bytes accessed | tf_op | source)
XLA Modules:
  0.0 215.8 jit_solution(1620051530298677860)
XLA Ops:
  0.6 0.0 copy-start
  0.6 33.3 %all_to_all.15.g_ref = bf16[8,256,256]{2,1,0:T(8,128)(2,1)} all-to-all(bf16[8,256,256]{2,1,0:T(8,128)(2,1)} %bitcast.8), channel_id=1, replica_groups=mesh['seq'=8,'ch'=4] {'seq'}, dimensions={0} | all-to-all | bytes 2097152 | tf_op jit(solution)/shard_map/all_to_all | solution.py:283
  33.9 3.6 %all-to-all-start = ((bf16[8,256,256]{2,1,0:T(8,128)(2,1)}), bf16[8,256,256]{2,1,0:T(8,128)(2,1)S(1)}, u32[]{:S(2)}, u32[]{:S(2)}) async-start(bf16[8,256,256]{2,1,0:T(8,128)(2,1)} %bitcast), calls=%async_computation | async-start | bytes 2097152 | tf_op jit(solution)/shard_map/all_to_all | solution.py:282
  37.5 1.6 multiply_reduce_fusion
  39.1 79.2 %all-gather.1 = f32[32,1,256]{2,1,0:T(1,128)S(1)} all-gather(f32[1,1,256]{2,1,0:T(1,128)S(1)} %bitcast.11), channel_id=2, replica_groups=mesh['seq'=8,'ch'=4] {'ch','seq'}, dimensions={0}, use_global_device_ids=true | all-gather | bytes 33792 | tf_op jit(solution)/shard_map/all_gather | solution.py:268
  118.3 0.1 reduce
  118.4 0.8 dynamic_slice.9
  119.1 0.7 constant_dynamic-slice_fusion.1
  119.8 0.1 copy.28
  120.0 0.8 copy.26.gain_ref
  120.8 0.6 pad.4.short_ref
  121.4 0.0 copy-done
  121.4 0.6 constant_dynamic-slice_fusion.medium_ref
  122.1 0.6 add_rsqrt_fusion
  122.7 0.0 all-to-all-done.x_ref
  122.7 0.0 copy-start.1
  122.7 1.0 copy-done.1
  123.6 63.7 %shard_map.183 = (bf16[8,256,256]{2,1,0:T(8,128)(2,1)}, f32[256,2048]{1,0:T(8,128)}, f32[256,128]{1,0:T(8,128)}, f32[256,128]{1,0:T(8,128)}) custom-call(bf16[8,256,256]{2,1,0:T(8,128)(2,1)} %copy-done.1, bf16[8,256,256]{2,1,0:T(8,128)(2,1)} %all_to_all.15.g_ref, f32[256,2048]{1,0:T(8,128)} %h_ref.1, f32[1,2048]{1,0:T(1,128)} %bitcast.10, ...), custom_call_target="tpu_custom_call" | custom-call | tf_op jit(solution)/shard_map/pallas_call | solution.py:229
  187.3 0.0 copy-start.2
  187.3 3.7 %all-to-all-start.2 = ((bf16[8,256,256]{2,1,0:T(8,128)(2,1)}), bf16[8,256,256]{2,1,0:T(8,128)(2,1)S(1)}, u32[]{:S(2)}, u32[]{:S(2)}) async-start(bf16[8,256,256]{2,1,0:T(8,128)(2,1)} %get-tuple-element.8), calls=%async_computation.2 | async-start | bytes 2097152 | tf_op jit(solution)/shard_map/all_to_all | solution.py:287
  191.0 0.0 copy-done.2
  191.1 0.7 copy.27
  191.7 23.1 %all-to-all-done.2 = bf16[8,256,256]{2,1,0:T(8,128)(2,1)S(1)} async-done(((bf16[8,256,256]{2,1,0:T(8,128)(2,1)}), bf16[8,256,256]{2,1,0:T(8,128)(2,1)S(1)}, u32[]{:S(2)}, u32[]{:S(2)}) %all-to-all-start.2) | async-done | bytes 1048608 | tf_op jit(solution)/shard_map/all_to_all | solution.py:287
  214.8 1.0 copy.30
  (2 shorter events, 0.0 us)
Async XLA Ops:
  0.6 120.8 %copy-start = (bf16[2048,128]{1,0:T(8,128)(2,1)S(1)}, bf16[2048,128]{1,0:T(8,128)(2,1)}, u32[]{:S(2)}) copy-start(bf16[2048,128]{1,0:T(8,128)(2,1)} %param.19) | copy-start | bytes 1572868
  33.9 88.8 %all-to-all-start = ((bf16[8,256,256]{2,1,0:T(8,128)(2,1)}), bf16[8,256,256]{2,1,0:T(8,128)(2,1)S(1)}, u32[]{:S(2)}, u32[]{:S(2)}) async-start(bf16[8,256,256]{2,1,0:T(8,128)(2,1)} %bitcast), calls=%async_computation | async-start | bytes 2097152 | tf_op jit(solution)/shard_map/all_to_all | solution.py:282
  122.7 1.0 copy-start.1
  187.3 3.7 %copy-start.2 = (f32[256,128]{1,0:T(8,128)S(1)}, f32[256,128]{1,0:T(8,128)}, u32[]{:S(2)}) copy-start(f32[256,128]{1,0:T(8,128)} %get-tuple-element.11) | copy-start | bytes 393220
  187.3 27.5 %all-to-all-start.2 = ((bf16[8,256,256]{2,1,0:T(8,128)(2,1)}), bf16[8,256,256]{2,1,0:T(8,128)(2,1)S(1)}, u32[]{:S(2)}, u32[]{:S(2)}) async-start(bf16[8,256,256]{2,1,0:T(8,128)(2,1)} %get-tuple-element.8), calls=%async_computation.2 | async-start | bytes 2097152 | tf_op jit(solution)/shard_map/all_to_all | solution.py:287

commit v2 on v1

v2 whole, which is shorter than its diff:
```python
import functools
import math

import jax
import jax.numpy as jnp
import ml_dtypes
import numpy as np
from jax import lax
from jax.experimental import pallas as pl
from jax.experimental.pallas import tpu as pltpu
from jax.sharding import PartitionSpec as P

LANES = 128
ROWS = 16
SIZE = 64


def halves(table):
    high = table.astype(np.float32).astype(ml_dtypes.bfloat16)
    low = (table - high.astype(np.float64)).astype(np.float32).astype(ml_dtypes.bfloat16)
    return high, low


@functools.lru_cache(maxsize=None)
def tables(blocks):
    outer = blocks + 1
    k = np.arange(outer)[:, None]
    a = np.arange(blocks)[None, :]
    q = np.arange(LANES)
    angle = 2.0 * math.pi * ((4 * k + 1) * a % (4 * outer)) / (4.0 * outer)
    eye = np.eye(ROWS)
    split = np.stack([np.cos(angle), -np.sin(angle)])
    ahead = np.einsum("xka,cd->xkcad", split, eye)
    ahead = ahead.reshape(2 * outer * ROWS, blocks * ROWS)
    back = ahead.T
    twist = 2.0 * math.pi * (4 * k + 1) * q[None, :] / (4.0 * outer * LANES)
    twist_re = np.repeat(np.cos(twist), ROWS, axis=0).astype(np.float32)
    twist_im = np.repeat(-np.sin(twist), ROWS, axis=0).astype(np.float32)
    inner = 2.0 * math.pi * (q[:, None] * q[None, :] % LANES) / LANES
    cos, sin = np.cos(inner), np.sin(inner)
    turn = np.block([[cos, -sin], [sin, cos]])
    return (
        *halves(ahead),
        *halves(back),
        twist_re,
        twist_im,
        *halves(turn),
        *halves(turn.T),
    )


def times(a, b):
    return (a[0] * b[0] - a[1] * b[1], a[0] * b[1] + a[1] * b[0])


def times_conj(a, b):
    return (a[0] * b[0] + a[1] * b[1], a[1] * b[0] - a[0] * b[1])


def dot(a, b):
    return jnp.dot(a, b, preferred_element_type=jnp.float32)


def parted(value):
    high = value.astype(jnp.bfloat16)
    return high, (value - high.astype(jnp.float32)).astype(jnp.bfloat16)


def fused_kernel(
    blocks,
    size,
    chunks,
    total_chans,
    x_ref,
    g_ref,
    h_ref,
    gain_ref,
    short_ref,
    medium_ref,
    ahead_hi,
    ahead_lo,
    back_hi,
    back_lo,
    twist_re,
    twist_im,
    turn_hi,
    turn_lo,
    turn_back_hi,
    turn_back_lo,
    normed_out,
    long_out,
    medium_out,
    short_out,
    normed_ref,
    x_in,
    g_in,
    leaving,
    squares,
    first,
    last_hi,
    last_lo,
    send_sem,
    recv_sem,
    square_send,
    square_recv,
):
    seq_count, group_chans, tokens = x_in.shape
    ch_count = squares.shape[0]
    me = lax.axis_index("seq")
    my_ch = lax.axis_index("ch")
    outer = blocks + 1
    groups = size // ROWS
    per = tokens // LANES
    half = outer * ROWS
    scale = 1.0 / (outer * LANES)
    root = (blocks * LANES) ** (-0.5)

    barrier = pltpu.get_barrier_semaphore()
    for d in range(1, seq_count):
        pl.semaphore_signal(
            barrier,
            inc=1,
            device_id={"seq": lax.rem(me + d, seq_count)},
            device_id_type=pl.DeviceIdType.MESH,
        )
    for d in range(1, ch_count):
        pl.semaphore_signal(
            barrier,
            inc=1,
            device_id={"ch": lax.rem(my_ch + d, ch_count)},
            device_id_type=pl.DeviceIdType.MESH,
        )
    pl.semaphore_wait(barrier, seq_count + ch_count - 2)

    def aligned(row):
        return pl.multiple_of(row, ROWS)

    def inward(which, chunk, d):
        to = lax.rem(me + d, seq_count)
        source = (g_ref, normed_ref)[which]
        target = (g_in, x_in)[which]
        return pltpu.make_async_remote_copy(
            src_ref=source.at[pl.ds(aligned(to * group_chans + chunk * size), size)],
            dst_ref=target.at[me, pl.ds(aligned(chunk * size), size)],
            send_sem=send_sem.at[which, chunk, d],
            recv_sem=recv_sem.at[which, chunk, d],
            device_id={"seq": to},
            device_id_type=pl.DeviceIdType.MESH,
        )

    def outward(chunk, d):
        to = lax.rem(me + d, seq_count)
        return pltpu.make_async_remote_copy(
            src_ref=leaving.at[to, pl.ds(aligned(chunk * size), size)],
            dst_ref=normed_out.at[pl.ds(aligned(me * group_chans + chunk * size), size)],
            send_sem=send_sem.at[2, chunk, d],
            recv_sem=recv_sem.at[2, chunk, d],
            device_id={"seq": to},
            device_id_type=pl.DeviceIdType.MESH,
        )

    def square_copy(d):
        return pltpu.make_async_remote_copy(
            src_ref=squares.at[my_ch],
            dst_ref=squares.at[my_ch],
            send_sem=square_send.at[d],
            recv_sem=square_recv.at[d],
            device_id={"ch": lax.rem(my_ch + d, ch_count)},
            device_id_type=pl.DeviceIdType.MESH,
        )

    def each_partner(act):
        lax.fori_loop(1, seq_count, lambda d, none: act(d), None)

    each_partner(lambda d: inward(0, 0, d).start())
    my_rows = pl.ds(aligned(me * group_chans), group_chans)
    g_in[me] = g_ref[my_rows, :]

    step = 8 * ROWS

    def add_rows(i, total):
        value = x_ref[pl.ds(aligned(i * step), step), :].astype(jnp.float32)
        return total + jnp.sum((value * value).reshape(step // 8, 8, tokens), axis=0)

    squares[my_ch] = lax.fori_loop(
        0, x_ref.shape[0] // step, add_rows, jnp.zeros((8, tokens), jnp.float32)
    )
    for d in range(1, ch_count):
        square_copy(d).start()
    for d in range(1, ch_count):
        square_copy(d).wait()
    mean = jnp.sum(jnp.sum(squares[...], axis=0), axis=0, keepdims=True) / total_chans
    inv_rms = lax.rsqrt(mean + 1e-05)

    def prepare(chunk, none):
        def one(d, none):
            to = lax.rem(me + d, seq_count)
            at = pl.ds(aligned(to * group_chans + chunk * size), size)
            value = x_ref[at, :].astype(jnp.float32) * inv_rms * gain_ref[at, :]
            normed_ref[at, :] = value.astype(jnp.bfloat16)

            @pl.when(d > 0)
            def _():
                inward(1, chunk, d).start()

        lax.fori_loop(0, seq_count, one, None)

        @pl.when(chunk + 1 < chunks)
        def _():
            each_partner(lambda d: inward(0, chunk + 1, d).start())

    lax.fori_loop(0, chunks, prepare, None)
    x_in[me] = normed_ref[my_rows, :]

    def work(chunk, none):
        def arrive(d):
            inward(0, chunk, d).wait_recv()
            inward(1, chunk, d).wait_recv()

        each_partner(arrive)
        local = chunk * size
        mine = me * group_chans + local

        def rows_at(start, group):
            return pl.ds(aligned(start + group * ROWS), ROWS)

        def piece(ref, group, block):
            lanes = slice((block % per) * LANES, (block % per + 1) * LANES)
            return ref[block // per, rows_at(local, group), lanes]

        for group in range(groups):
            lanes = slice(group * LANES, (group + 1) * LANES)
            rows = rows_at(local, group)
            normed = jnp.concatenate([piece(x_in, group, b) for b in range(blocks)], axis=0)
            grads = jnp.concatenate([piece(g_in, group, b) for b in range(blocks)], axis=0)
            taps = jnp.concatenate(
                [h_ref[rows, b * LANES : (b + 1) * LANES] for b in range(blocks)], axis=0
            )
            taps_hi, taps_lo = parted(taps)
            pair = jnp.concatenate([normed, grads], axis=1)
            both = dot(ahead_hi[...], pair) + dot(ahead_lo[...], pair)
            first[0, :, lanes] = both[:, :LANES]
            first[1, :, lanes] = both[:, LANES:]
            pair = jnp.concatenate([taps_hi, taps_lo], axis=1)
            both = dot(ahead_hi[...], pair)
            first[2, :, lanes] = both[:, :LANES] + both[:, LANES:] + dot(ahead_lo[...], taps_hi)

        def at_freq(k, sums):
            top = pl.multiple_of(k * ROWS, ROWS)
            bottom = pl.multiple_of(half + k * ROWS, ROWS)
            t_re = twist_re[pl.ds(top, ROWS), :]
            t_im = twist_im[pl.ds(top, ROWS), :]
            stack = []
            for signal in range(3):
                for group in range(groups):
                    lanes = slice(group * LANES, (group + 1) * LANES)
                    value = (
                        first[signal, pl.ds(top, ROWS), lanes],
                        first[signal, pl.ds(bottom, ROWS), lanes],
                    )
                    stack.append(jnp.concatenate(times(value, (t_re, t_im)), axis=1))
            for ref, start in ((short_ref, local), (medium_ref, mine)):
                for group in range(groups):
                    taps = ref[rows_at(start, group), :].astype(jnp.float32)
                    stack.append(jnp.concatenate([taps * t_re, taps * t_im], axis=1))
            high, low = parted(jnp.concatenate(stack, axis=0))
            spec = dot(high, turn_hi[...]) + dot(low, turn_hi[...]) + dot(high, turn_lo[...])
            count = groups * ROWS
            normed, grads, taps, short, medium = [
                (spec[i * count : (i + 1) * count, :LANES], spec[i * count : (i + 1) * count, LANES:])
                for i in range(5)
            ]
            shorted = times(short, normed)
            grad_long = times_conj(grads, times(medium, shorted))
            grad_filtered = times_conj(grads, taps)
            grad_medium = times_conj(grad_filtered, shorted)
            grad_shorted = times_conj(grad_filtered, medium)
            grad_short = times_conj(grad_shorted, normed)
            grad_normed = times_conj(grad_shorted, short)
            stack = [
                jnp.concatenate(value, axis=1)
                for value in (grad_normed, grad_long, grad_medium, grad_short)
            ]
            high, low = parted(jnp.concatenate(stack, axis=0))
            step = (
                dot(high, turn_back_hi[...])
                + dot(low, turn_back_hi[...])
                + dot(high, turn_back_lo[...])
            )
            for signal in range(2):
                for group in range(groups):
                    at = signal * count + group * ROWS
                    lanes = slice(group * LANES, (group + 1) * LANES)
                    value = (step[at : at + ROWS, :LANES], step[at : at + ROWS, LANES:])
                    turned = times_conj(value, (t_re, t_im))
                    for where, part in zip((top, bottom), turned):
                        part_hi, part_lo = parted(part)
                        last_hi[signal, pl.ds(where, ROWS), lanes] = part_hi
                        last_lo[signal, pl.ds(where, ROWS), lanes] = part_lo
            result = []
            for signal in range(2):
                for group in range(groups):
                    at = (2 + signal) * count + group * ROWS
                    real = step[at : at + ROWS, :LANES] * t_re + step[at : at + ROWS, LANES:] * t_im
                    result.append(sums[signal * groups + group] + real)
            return tuple(result)

        zero = jnp.zeros((ROWS, LANES), jnp.float32)
        sums = lax.fori_loop(0, outer, at_freq, (zero,) * (2 * groups))
        for signal in range(2):
            value = (
                dot(back_hi[...], last_hi[signal])
                + dot(back_hi[...], last_lo[signal])
                + dot(back_lo[...], last_hi[signal])
            )
            for group in range(groups):
                rows = rows_at(local, group)
                for block in range(blocks):
                    part = value[
                        block * ROWS : (block + 1) * ROWS, group * LANES : (group + 1) * LANES
                    ]
                    lanes = slice((block % per) * LANES, (block % per + 1) * LANES)
                    if signal == 0:
                        leaving[block // per, rows, lanes] = (part * scale).astype(jnp.bfloat16)
                    else:
                        long_out[rows, block * LANES : (block + 1) * LANES] = part * (scale * root)
            if signal == 0:
                each_partner(lambda d: outward(chunk, d).start())
        for group in range(groups):
            rows = rows_at(local, group)
            medium_out[rows, :] = sums[group] * (scale * root)
            short_out[rows, :] = sums[groups + group] * (scale * root)

    lax.fori_loop(0, chunks, work, None)
    normed_out[my_rows, :] = leaving[me]

    def finish(chunk, none):
        def one(d):
            inward(0, chunk, d).wait_send()
            inward(1, chunk, d).wait_send()
            outward(chunk, d).wait()

        each_partner(one)

    lax.fori_loop(0, chunks, finish, None)


def on_device(block_input, norm_gain, short_taps, medium_taps, long_filter, grad_out):
    chans, tokens = block_input.shape
    seq_count = lax.axis_size("seq")
    ch_count = lax.axis_size("ch")
    group = chans // seq_count
    length = seq_count * tokens
    short_count = short_taps.shape[1]
    blocks = length // LANES
    outer = blocks + 1
    size = min(group, SIZE if blocks <= 16 else ROWS)
    chunks = group // size
    offset = lax.axis_index("seq") * group
    short = lax.dynamic_slice_in_dim(short_taps, offset, group, 0)
    short = jnp.pad(short, ((0, 0), (0, LANES - short_count)))
    consts = [jnp.asarray(t) for t in tables(blocks)]
    vmem = pl.BlockSpec(memory_space=pltpu.VMEM)
    lanes = size // ROWS * LANES
    normed, long, med, sho = pl.pallas_call(
        functools.partial(fused_kernel, blocks, size, chunks, chans * ch_count),
        in_specs=[vmem] * (6 + len(consts)),
        out_specs=[vmem] * 4,
        out_shape=[
            jax.ShapeDtypeStruct((chans, tokens), jnp.bfloat16),
            jax.ShapeDtypeStruct((group, length), jnp.float32),
            jax.ShapeDtypeStruct((group, LANES), jnp.float32),
            jax.ShapeDtypeStruct((group, LANES), jnp.float32),
        ],
        scratch_shapes=[
            pltpu.VMEM((chans, tokens), jnp.bfloat16),
            pltpu.VMEM((seq_count, group, tokens), jnp.bfloat16),
            pltpu.VMEM((seq_count, group, tokens), jnp.bfloat16),
            pltpu.VMEM((seq_count, group, tokens), jnp.bfloat16),
            pltpu.VMEM((ch_count, 8, tokens), jnp.float32),
            pltpu.VMEM((3, 2 * outer * ROWS, lanes), jnp.float32),
            pltpu.VMEM((2, 2 * outer * ROWS, lanes), jnp.bfloat16),
            pltpu.VMEM((2, 2 * outer * ROWS, lanes), jnp.bfloat16),
            pltpu.SemaphoreType.DMA((3, chunks, seq_count)),
            pltpu.SemaphoreType.DMA((3, chunks, seq_count)),
            pltpu.SemaphoreType.DMA((ch_count,)),
            pltpu.SemaphoreType.DMA((ch_count,)),
        ],
        compiler_params=pltpu.CompilerParams(
            vmem_limit_bytes=58 * 1024 * 1024, collective_id=0, has_side_effects=True
        ),
    )(block_input, grad_out, long_filter, norm_gain[:, None], short, medium_taps, *consts)
    return (normed, long, med[:, : medium_taps.shape[1]], sho[:, :short_count])


def solution(mesh):
    placed = (
        P("ch", "seq"),
        P("ch"),
        P("ch", None),
        P("ch", None),
        P(("ch", "seq"), None),
        P("ch", "seq"),
    )
    return jax.shard_map(
        on_device,
        mesh=mesh,
        in_specs=placed,
        out_specs=(
            P("ch", "seq"),
            P(("ch", "seq"), None),
            P(("ch", "seq"), None),
            P(("ch", "seq"), None),
        ),
        check_vma=False,
    )
```

time: 216 us -> 108 us (0.50)
  blocking collectives: 112 us -> 0 us
  Pallas kernels: 63.7 us -> 97.4 us
  waiting for transfers between devices: 23.1 us -> 0 us
  starting transfers between devices: 7.29 us -> 0 us
  local copies, waits for them, and re-layouts: 6.3 us -> 9.55 us
  other arithmetic: 2.27 us -> 0 us
    all_gather x1 -> x0, blocking collectives: 79.2 us -> none  [on_device(): everyones = lax.all_gather(squares, ('ch', 'seq')).reshape(ch_count, length)]
    pallas_call x1, Pallas kernels: 63.7 us -> 97.4 us  [on_device(): pl.pallas_call(functools.partial(fused_kernel, blocks, size, chunks, chan...]
    all_to_all x1 -> x0, blocking collectives: 33.3 us -> none  [on_device(): lax.all_to_all(g_all[:, at], 'seq', split_axis=0, concat_axis=0, tiled=True)]
    all_to_all x2 -> x0, waiting for transfers between devices: 23.1 us -> none  [the longest x1 23.1 us: on_device(): lax.all_to_all(normed, 'seq', split_axis=0, concat_axis=0, tiled=True)]
    all_to_all x2 -> x0, starting transfers between devices: 7.29 us -> none  [the longest x1 3.7 us: on_device(): lax.all_to_all(normed, 'seq', split_axis=0, concat_axis=0, tiled=True)]
    unnamed x9 -> x11, local copies, waits for them, and re-layouts: 2.78 us -> 6.87 us
  transfers between devices with their start and end apart: 2 -> 0, of which waited for: 1 -> 0; matrix products, arithmetic and copies ran while one was open for 3% -> 0% of each run, Pallas kernels for 0% -> 0%
where the time goes in v2:
time: 108 us
  Pallas kernels  97.4 us (90%)
  local copies, waits for them, and re-layouts  9.55 us (9%)
    pallas_call x1, Pallas kernels, on_device(): pl.pallas_call(functools.partial(fused_kernel, blocks, size, chunks, chan...  97.4 us
    unnamed x11, local copies, waits for them, and re-layouts  6.87 us

profile of v2, /device:TPU:0, one launch (start us, length us, event | category | flops | bytes accessed | tf_op | source)
XLA Modules:
  0.0 107.6 jit_solution(17252343551344056877)
XLA Ops:
  0.6 0.0 copy-start
  0.7 0.7 copy-done
  1.4 0.1 copy.25
  1.5 0.6 pad.4.short_ref
  2.2 2.0 %copy.23.gain_ref = f32[2048,1]{1,0:T(8,128)} copy(f32[2048,1]{0,1:T(1,128)} %bitcast.3) | data formatting | bytes 16384 | tf_op jit(solution)/shard_map/broadcast_in_dim | solution.py:392
  4.2 97.4 %shard_map.183 = (bf16[2048,256]{1,0:T(8,128)(2,1)}, f32[256,2048]{1,0:T(8,128)}, f32[256,128]{1,0:T(8,128)}, f32[256,128]{1,0:T(8,128)}) custom-call(bf16[2048,256]{1,0:T(8,128)(2,1)} %x_ref.1, bf16[2048,256]{1,0:T(8,128)(2,1)} %g_ref.1, f32[256,2048]{1,0:T(8,128)} %h_ref.1, f32[2048,1]{1,0:T(8,128)} %copy.23.gain_ref, bf16[256,128]{1,0:T(8,128)(2,1)} %pad.4.short_ref, ...), custom_call_target="tpu_custom_call" | custom-call | tf_op jit(solution)/shard_map/pallas_call | solution.py:365
  101.6 0.0 copy-start.1
  101.6 1.7 %copy.24 = f32[256,7]{0,1:T(8,128)} copy(f32[256,7]{1,0:T(8,128)} %bitcast.2) | data formatting | bytes 14336
  103.3 2.3 %copy.29 = bf16[2048,256]{1,0:T(8,128)(2,1)} copy(bf16[2048,256]{1,0:T(8,128)(2,1)} %get-tuple-element.24) | data formatting | bytes 2097152
  105.6 0.0 copy-done.1
  105.6 0.0 copy-start.2
  105.6 1.3 %copy.30 = f32[256,2048]{1,0:T(8,128)} copy(f32[256,2048]{1,0:T(8,128)S(1)} %copy-done.1) | data formatting | bytes 4194304
  106.9 0.0 copy-done.2
  106.9 0.7 copy.31
  (1 shorter events, 0.0 us)
Async XLA Ops:
  0.6 0.8 copy-start
  101.6 4.0 %copy-start.1 = (f32[256,2048]{1,0:T(8,128)S(1)}, f32[256,2048]{1,0:T(8,128)}, u32[]{:S(2)}) copy-start(f32[256,2048]{1,0:T(8,128)} %get-tuple-element.25) | copy-start | bytes 6291460
  105.6 1.3 %copy-start.2 = (f32[256,128]{1,0:T(8,128)S(1)}, f32[256,128]{1,0:T(8,128)}, u32[]{:S(2)}) copy-start(f32[256,128]{1,0:T(8,128)} %get-tuple-element.26) | copy-start | bytes 393220

commit v3 on v2

--- a/solution.py
+++ b/solution.py
@@ -13,6 +13,7 @@
 LANES = 128
 ROWS = 16
 SIZE = 64
+FREQS = 4
 
 
 def halves(table):
@@ -41,11 +42,11 @@
     turn = np.block([[cos, -sin], [sin, cos]])
     return (
         *halves(ahead),
-        *halves(back),
+        halves(back)[0],
         twist_re,
         twist_im,
         *halves(turn),
-        *halves(turn.T),
+        halves(turn.T)[0],
     )
 
 
@@ -80,22 +81,22 @@
     ahead_hi,
     ahead_lo,
     back_hi,
-    back_lo,
     twist_re,
     twist_im,
     turn_hi,
     turn_lo,
     turn_back_hi,
-    turn_back_lo,
     normed_out,
     long_out,
     medium_out,
     short_out,
+    gain_rows,
     normed_ref,
     x_in,
     g_in,
     leaving,
     squares,
+    h_in,
     first,
     last_hi,
     last_lo,
@@ -103,6 +104,7 @@
     recv_sem,
     square_send,
     square_recv,
+    fetch_sem,
 ):
     seq_count, group_chans, tokens = x_in.shape
     ch_count = squares.shape[0]
@@ -173,6 +175,8 @@
         lax.fori_loop(1, seq_count, lambda d, none: act(d), None)
 
     each_partner(lambda d: inward(0, 0, d).start())
+    fetch = pltpu.make_async_copy(h_ref, h_in, fetch_sem)
+    fetch.start()
     my_rows = pl.ds(aligned(me * group_chans), group_chans)
     g_in[me] = g_ref[my_rows, :]
 
@@ -187,6 +191,12 @@
     )
     for d in range(1, ch_count):
         square_copy(d).start()
+
+    def spread(i, none):
+        wide = jnp.broadcast_to(gain_ref[pl.ds(i, 1), :], (LANES, LANES))
+        gain_rows[pl.ds(aligned(i * LANES), LANES), :] = wide.T
+
+    lax.fori_loop(0, gain_ref.shape[0], spread, None)
     for d in range(1, ch_count):
         square_copy(d).wait()
     mean = jnp.sum(jnp.sum(squares[...], axis=0), axis=0, keepdims=True) / total_chans
@@ -196,7 +206,8 @@
         def one(d, none):
             to = lax.rem(me + d, seq_count)
             at = pl.ds(aligned(to * group_chans + chunk * size), size)
-            value = x_ref[at, :].astype(jnp.float32) * inv_rms * gain_ref[at, :]
+            gain = jnp.concatenate([gain_rows[at, :]] * per, axis=1)
+            value = x_ref[at, :].astype(jnp.float32) * inv_rms * gain
             normed_ref[at, :] = value.astype(jnp.bfloat16)
 
             @pl.when(d > 0)
@@ -211,6 +222,7 @@
 
     lax.fori_loop(0, chunks, prepare, None)
     x_in[me] = normed_ref[my_rows, :]
+    fetch.wait()
 
     def work(chunk, none):
         def arrive(d):
@@ -234,7 +246,7 @@
             normed = jnp.concatenate([piece(x_in, group, b) for b in range(blocks)], axis=0)
             grads = jnp.concatenate([piece(g_in, group, b) for b in range(blocks)], axis=0)
             taps = jnp.concatenate(
-                [h_ref[rows, b * LANES : (b + 1) * LANES] for b in range(blocks)], axis=0
+                [h_in[rows, b * LANES : (b + 1) * LANES] for b in range(blocks)], axis=0
             )
             taps_hi, taps_lo = parted(taps)
             pair = jnp.concatenate([normed, grads], axis=1)
@@ -245,73 +257,79 @@
             both = dot(ahead_hi[...], pair)
             first[2, :, lanes] = both[:, :LANES] + both[:, LANES:] + dot(ahead_lo[...], taps_hi)
 
-        def at_freq(k, sums):
-            top = pl.multiple_of(k * ROWS, ROWS)
-            bottom = pl.multiple_of(half + k * ROWS, ROWS)
-            t_re = twist_re[pl.ds(top, ROWS), :]
-            t_im = twist_im[pl.ds(top, ROWS), :]
+        def at_freqs(start, width, sums):
             stack = []
-            for signal in range(3):
-                for group in range(groups):
-                    lanes = slice(group * LANES, (group + 1) * LANES)
-                    value = (
-                        first[signal, pl.ds(top, ROWS), lanes],
-                        first[signal, pl.ds(bottom, ROWS), lanes],
-                    )
-                    stack.append(jnp.concatenate(times(value, (t_re, t_im)), axis=1))
-            for ref, start in ((short_ref, local), (medium_ref, mine)):
-                for group in range(groups):
-                    taps = ref[rows_at(start, group), :].astype(jnp.float32)
-                    stack.append(jnp.concatenate([taps * t_re, taps * t_im], axis=1))
+            places = []
+            for k in range(width):
+                top = aligned((start + k) * ROWS)
+                bottom = aligned(half + (start + k) * ROWS)
+                t_re = twist_re[pl.ds(top, ROWS), :]
+                t_im = twist_im[pl.ds(top, ROWS), :]
+                places.append((top, bottom, t_re, t_im))
+                for signal in range(3):
+                    for group in range(groups):
+                        lanes = slice(group * LANES, (group + 1) * LANES)
+                        value = (
+                            first[signal, pl.ds(top, ROWS), lanes],
+                            first[signal, pl.ds(bottom, ROWS), lanes],
+                        )
+                        stack.append(jnp.concatenate(times(value, (t_re, t_im)), axis=1))
+                for ref, begin in ((short_ref, local), (medium_ref, mine)):
+                    for group in range(groups):
+                        taps = ref[rows_at(begin, group), :].astype(jnp.float32)
+                        stack.append(jnp.concatenate([taps * t_re, taps * t_im], axis=1))
             high, low = parted(jnp.concatenate(stack, axis=0))
             spec = dot(high, turn_hi[...]) + dot(low, turn_hi[...]) + dot(high, turn_lo[...])
             count = groups * ROWS
-            normed, grads, taps, short, medium = [
-                (spec[i * count : (i + 1) * count, :LANES], spec[i * count : (i + 1) * count, LANES:])
-                for i in range(5)
-            ]
-            shorted = times(short, normed)
-            grad_long = times_conj(grads, times(medium, shorted))
-            grad_filtered = times_conj(grads, taps)
-            grad_medium = times_conj(grad_filtered, shorted)
-            grad_shorted = times_conj(grad_filtered, medium)
-            grad_short = times_conj(grad_shorted, normed)
-            grad_normed = times_conj(grad_shorted, short)
-            stack = [
-                jnp.concatenate(value, axis=1)
-                for value in (grad_normed, grad_long, grad_medium, grad_short)
-            ]
+            stack = []
+            for k in range(width):
+                normed, grads, taps, short, medium = [
+                    (spec[i * count : (i + 1) * count, :LANES], spec[i * count : (i + 1) * count, LANES:])
+                    for i in range(5 * k, 5 * k + 5)
+                ]
+                shorted = times(short, normed)
+                grad_long = times_conj(grads, times(medium, shorted))
+                grad_filtered = times_conj(grads, taps)
+                grad_medium = times_conj(grad_filtered, shorted)
+                grad_shorted = times_conj(grad_filtered, medium)
+                grad_short = times_conj(grad_shorted, normed)
+                grad_normed = times_conj(grad_shorted, short)
+                stack += [
+                    jnp.concatenate(value, axis=1)
+                    for value in (grad_normed, grad_long, grad_medium, grad_short)
+                ]
             high, low = parted(jnp.concatenate(stack, axis=0))
             step = (
                 dot(high, turn_back_hi[...])
                 + dot(low, turn_back_hi[...])
-                + dot(high, turn_back_lo[...])
             )
-            for signal in range(2):
-                for group in range(groups):
-                    at = signal * count + group * ROWS
-                    lanes = slice(group * LANES, (group + 1) * LANES)
-                    value = (step[at : at + ROWS, :LANES], step[at : at + ROWS, LANES:])
-                    turned = times_conj(value, (t_re, t_im))
-                    for where, part in zip((top, bottom), turned):
-                        part_hi, part_lo = parted(part)
-                        last_hi[signal, pl.ds(where, ROWS), lanes] = part_hi
-                        last_lo[signal, pl.ds(where, ROWS), lanes] = part_lo
-            result = []
-            for signal in range(2):
-                for group in range(groups):
-                    at = (2 + signal) * count + group * ROWS
-                    real = step[at : at + ROWS, :LANES] * t_re + step[at : at + ROWS, LANES:] * t_im
-                    result.append(sums[signal * groups + group] + real)
-            return tuple(result)
+            sums = list(sums)
+            for k, (top, bottom, t_re, t_im) in enumerate(places):
+                for signal in range(4):
+                    for group in range(groups):
+                        at = (4 * k + signal) * count + group * ROWS
+                        value = (step[at : at + ROWS, :LANES], step[at : at + ROWS, LANES:])
+                        if signal >= 2:
+                            real = value[0] * t_re + value[1] * t_im
+                            sums[(signal - 2) * groups + group] += real
+                            continue
+                        lanes = slice(group * LANES, (group + 1) * LANES)
+                        turned = times_conj(value, (t_re, t_im))
+                        for where, part in zip((top, bottom), turned):
+                            part_hi, part_lo = parted(part)
+                            last_hi[signal, pl.ds(where, ROWS), lanes] = part_hi
+                            last_lo[signal, pl.ds(where, ROWS), lanes] = part_lo
+            return tuple(sums)
 
         zero = jnp.zeros((ROWS, LANES), jnp.float32)
-        sums = lax.fori_loop(0, outer, at_freq, (zero,) * (2 * groups))
+        sums = at_freqs(0, 1, (zero,) * (2 * groups))
+        sums = lax.fori_loop(
+            0, blocks // FREQS, lambda i, s: at_freqs(1 + i * FREQS, FREQS, s), sums
+        )
         for signal in range(2):
             value = (
                 dot(back_hi[...], last_hi[signal])
                 + dot(back_hi[...], last_lo[signal])
-                + dot(back_lo[...], last_hi[signal])
             )
             for group in range(groups):
                 rows = rows_at(local, group)
@@ -364,7 +382,7 @@
     lanes = size // ROWS * LANES
     normed, long, med, sho = pl.pallas_call(
         functools.partial(fused_kernel, blocks, size, chunks, chans * ch_count),
-        in_specs=[vmem] * (6 + len(consts)),
+        in_specs=[vmem] * 2 + [pl.BlockSpec(memory_space=pl.ANY)] + [vmem] * (3 + len(consts)),
         out_specs=[vmem] * 4,
         out_shape=[
             jax.ShapeDtypeStruct((chans, tokens), jnp.bfloat16),
@@ -373,11 +391,13 @@
             jax.ShapeDtypeStruct((group, LANES), jnp.float32),
         ],
         scratch_shapes=[
+            pltpu.VMEM((chans, LANES), jnp.float32),
             pltpu.VMEM((chans, tokens), jnp.bfloat16),
             pltpu.VMEM((seq_count, group, tokens), jnp.bfloat16),
             pltpu.VMEM((seq_count, group, tokens), jnp.bfloat16),
             pltpu.VMEM((seq_count, group, tokens), jnp.bfloat16),
             pltpu.VMEM((ch_count, 8, tokens), jnp.float32),
+            pltpu.VMEM((group, length), jnp.float32),
             pltpu.VMEM((3, 2 * outer * ROWS, lanes), jnp.float32),
             pltpu.VMEM((2, 2 * outer * ROWS, lanes), jnp.bfloat16),
             pltpu.VMEM((2, 2 * outer * ROWS, lanes), jnp.bfloat16),
@@ -385,11 +405,12 @@
             pltpu.SemaphoreType.DMA((3, chunks, seq_count)),
             pltpu.SemaphoreType.DMA((ch_count,)),
             pltpu.SemaphoreType.DMA((ch_count,)),
+            pltpu.SemaphoreType.DMA,
         ],
         compiler_params=pltpu.CompilerParams(
             vmem_limit_bytes=58 * 1024 * 1024, collective_id=0, has_side_effects=True
         ),
-    )(block_input, grad_out, long_filter, norm_gain[:, None], short, medium_taps, *consts)
+    )(block_input, grad_out, long_filter, norm_gain.reshape(-1, LANES), short, medium_taps, *consts)
     return (normed, long, med[:, : medium_taps.shape[1]], sho[:, :short_count])
 
 

time: 108 us -> 89.4 us (0.83)
  Pallas kernels: 97.4 us -> 81 us
  local copies, waits for them, and re-layouts: 9.55 us -> 7.52 us
    pallas_call x1, Pallas kernels: 97.4 us -> 81 us  [on_device(): pl.pallas_call(functools.partial(fused_kernel, blocks, size, chunks, chan...]
    broadcast_in_dim x1 -> x0, local copies, waits for them, and re-layouts: 2.04 us -> none  [on_device(): norm_gain[:, None]]
where the time goes in v3:
time: 89.4 us; the launch traced here: 89.1 us
  Pallas kernels  81 us (91%)
  local copies, waits for them, and re-layouts  7.52 us (8%)
    pallas_call x1, Pallas kernels, on_device(): pl.pallas_call(functools.partial(fused_kernel, blocks, size, chunks, chan...  81 us
    unnamed x11, local copies, waits for them, and re-layouts  6.87 us

profile of v3, /device:TPU:0, one launch (start us, length us, event | category | flops | bytes accessed | tf_op | source)
XLA Modules:
  0.0 89.1 jit_solution(6954640310053587654)
XLA Ops:
  0.6 0.0 copy-start
  0.7 0.7 copy-done
  1.4 0.1 copy.20
  1.5 0.6 pad.4.short_ref
  2.2 81.0 %shard_map.165 = (bf16[2048,256]{1,0:T(8,128)(2,1)}, f32[256,2048]{1,0:T(8,128)}, f32[256,128]{1,0:T(8,128)}, f32[256,128]{1,0:T(8,128)}) custom-call(bf16[2048,256]{1,0:T(8,128)(2,1)} %x_ref.1, bf16[2048,256]{1,0:T(8,128)(2,1)} %g_ref.1, f32[256,2048]{1,0:T(8,128)} %h_ref.1, f32[16,128]{1,0:T(8,128)} %bitcast.3, bf16[256,128]{1,0:T(8,128)(2,1)} %pad.4.short_ref, ...), custom_call_target="tpu_custom_call" | custom-call | tf_op jit(solution)/shard_map/pallas_call | solution.py:383
  83.2 0.0 copy-start.1
  83.2 1.7 %copy.19 = f32[256,7]{0,1:T(8,128)} copy(f32[256,7]{1,0:T(8,128)} %bitcast.2) | data formatting | bytes 14336
  84.9 2.3 %copy.24 = bf16[2048,256]{1,0:T(8,128)(2,1)} copy(bf16[2048,256]{1,0:T(8,128)(2,1)} %get-tuple-element.20) | data formatting | bytes 2097152
  87.2 0.0 copy-done.1
  87.2 0.0 copy-start.2
  87.2 1.3 %copy.25 = f32[256,2048]{1,0:T(8,128)} copy(f32[256,2048]{1,0:T(8,128)S(1)} %copy-done.1) | data formatting | bytes 4194304
  88.5 0.0 copy-done.2
  88.5 0.7 copy.26
  (1 shorter events, 0.0 us)
Async XLA Ops:
  0.6 0.8 copy-start
  83.2 4.0 %copy-start.1 = (f32[256,2048]{1,0:T(8,128)S(1)}, f32[256,2048]{1,0:T(8,128)}, u32[]{:S(2)}) copy-start(f32[256,2048]{1,0:T(8,128)} %get-tuple-element.21) | copy-start | bytes 6291460
  87.2 1.3 %copy-start.2 = (f32[256,128]{1,0:T(8,128)S(1)}, f32[256,128]{1,0:T(8,128)}, u32[]{:S(2)}) copy-start(f32[256,128]{1,0:T(8,128)} %get-tuple-element.22) | copy-start | bytes 393220
